TPU v7x, 32 devices: a whole 2x2x4 slice. The times are simulated.
32 devices in a mesh: dp: 4 (over y, x), tensor: 8 (over z, core).
Axes of the slice: x: 2, y: 2, z: 4, core: 2. Of those that a mesh axis runs over, the one named last changes fastest.
Arguments:
- prefill_state: float32 [16, 256, 64, 128], P('dp', 'tensor'), may hold values from -1.2 to 1.2
- assign: int32 [16], replicated, may hold values from 0 to 15, as said below
- tokens: int32 [16, 2], replicated, may hold values from 0 to 65535
- embed_table: bfloat16 [65536, 8192], P('tensor', 'dp'), may hold values from -6 to 6
- w_xz: bfloat16 [8192, 256, 128], P('dp', 'tensor'), may hold values from -0.0625 to 0.0625
- w_dt: bfloat16 [8192, 256], P('dp', 'tensor'), may hold values from -0.0625 to 0.0625
- w_bc: bfloat16 [8192, 2048], P('dp', 'tensor'), may hold values from -0.0625 to 0.0625
- dt_bias: float32 [256], P('tensor'), may hold values from -3 to 0
- a_log: float32 [256], P('tensor'), may hold values from 0 to 1.5
- d_skip: float32 [256], P('tensor'), may hold values from 0.5 to 2
- norm_w: float32 [256, 64], P('tensor'), may hold values from 0.1 to 1.9
- w_out: bfloat16 [16384, 8192], P('tensor', 'dp'), may hold values from -0.046875 to 0.046875
Outputs:
- layer_out: bfloat16 [16, 2, 8192], P('tensor', None, 'dp')
- decode_state: float32 [4, 8, 64, 2, 64, 128], P('dp', 'tensor')
Inputs may be any that keep to these rules, and one draw needn't show every extreme that they name: assign is a permutation; the 4 requests i with i // 4 = s send exactly 1 to the positions p with p // 4 = d, for every s and d.
All inputs are finite; a program needn't handle non-finite values.
Results may differ from a plain program's by a relative error of at most 0.0041.
Values may be sent and summed in bfloat16 or wider, within the bound.
A program may use at most 256 MiB of HBM per device.

v0:
```python
import jax
import jax.numpy as jnp
from jax import lax
from jax.sharding import PartitionSpec as P

HEADS = 256
GROUPS = 8
RANKS = 4


norm_eps = 1e-05


def partner(value, axis, apart):
    mask = 2**apart
    pairs = [(source, source ^ mask) for source in range(lax.axis_size(axis))]
    return lax.ppermute(value, axis, pairs)


def arrange(value, quads, ranks):
    rest = value.shape[2:]
    group_req = value.shape[0] // quads
    rank_heads = value.shape[1] // ranks
    shaped = value.reshape((quads, group_req, ranks, rank_heads) + rest)
    extra = tuple(range(4, 4 + len(rest)))
    moved = jnp.transpose(shaped, (0, 2, 3, 1) + extra)
    return moved.reshape((quads * ranks, rank_heads, group_req) + rest)


def restore(value, quads, ranks):
    rank_heads = value.shape[1]
    group_req = value.shape[2]
    rest = value.shape[3:]
    shaped = value.reshape((quads, ranks, rank_heads, group_req) + rest)
    extra = tuple(range(4, 4 + len(rest)))
    moved = jnp.transpose(shaped, (0, 3, 1, 2) + extra)
    return moved.reshape((quads * group_req, ranks * rank_heads) + rest)


def advance(ssm_state, inputs, raw_dt, bc_rows, bias, decay_rate, skip):
    steps = raw_dt.shape[-1]
    head_dim = inputs.shape[-1] // 2
    state_dim = bc_rows.shape[-1] // 2
    results = []
    for step_idx in range(steps):
        xin = inputs[..., step_idx, :head_dim]
        zin = inputs[..., step_idx, head_dim:]
        bvec = bc_rows[..., step_idx, :state_dim]
        cvec = bc_rows[..., step_idx, state_dim:]
        delta = jax.nn.softplus(raw_dt[..., step_idx] + bias)
        decay = jnp.exp(-delta * decay_rate)
        ssm_state = (
            ssm_state * decay[..., None, None]
            + (delta[..., None] * xin)[..., :, None] * bvec[..., None, :]
        )
        yout = jnp.sum(ssm_state * cvec[..., None, :], axis=-1) + skip[..., None] * xin
        results.append(yout * jax.nn.silu(zin))
    return (ssm_state, jnp.stack(results, axis=-2))


def group_totals(partial_value, bit_count):
    for bit in range(bit_count):
        partial_value = partial_value + partner(partial_value, "tensor", bit)
    return partial_value


def to_groups(state, assign, dindex, ndp):
    req_dp = state.shape[0]
    pair = req_dp // ndp
    own_pos = lax.dynamic_slice_in_dim(assign, dindex * req_dp, req_dp)
    send_order = jnp.argsort(own_pos)
    outgoing = jnp.take(state, send_order, axis=0).reshape((ndp, pair) + state.shape[1:])
    incoming = lax.all_to_all(outgoing, "dp", split_axis=0, concat_axis=0, tiled=True)
    sorted_pos = jnp.sort(assign.reshape(ndp, req_dp), axis=1)
    arrived = lax.dynamic_slice_in_dim(sorted_pos, dindex * pair, pair, 1) - dindex * req_dp
    slot_order = jnp.argsort(arrived.reshape(-1))
    return jnp.take(incoming.reshape(state.shape), slot_order, axis=0)


def on_device(
    prefill_state,
    assign,
    tokens,
    embed_table,
    w_xz,
    w_dt,
    w_bc,
    dt_bias,
    a_log,
    d_skip,
    norm_w,
    w_out,
):
    ntensor = lax.axis_size("tensor")
    ndp = lax.axis_size("dp")
    tindex = lax.axis_index("tensor")
    dindex = lax.axis_index("dp")
    req_dp, heads_dev, head_dim, state_dim = prefill_state.shape
    requests = req_dp * ndp
    steps = tokens.shape[1]
    quads = ntensor // RANKS
    group_req = req_dp // quads
    rank_heads = heads_dev // RANKS
    per_group = HEADS // GROUPS
    state_heads = to_groups(prefill_state, assign, dindex, ndp)
    inverse = jnp.argsort(assign)
    tok_pos = jnp.take(tokens, inverse, axis=0)
    vocab_dev = embed_table.shape[0]
    local_ids = tok_pos - tindex * vocab_dev
    inside = (local_ids >= 0) & (local_ids < vocab_dev)
    looked = jnp.take(embed_table, jnp.clip(local_ids, 0, vocab_dev - 1), axis=0)
    terms = jnp.where(inside[..., None], looked.astype(jnp.float32), 0.0)
    emb_mine = lax.psum_scatter(
        terms.astype(jnp.bfloat16), "tensor", scatter_dimension=0, tiled=True
    ).astype(jnp.float32)
    emb_all = lax.all_gather(emb_mine.astype(jnp.bfloat16), "tensor", axis=0, tiled=True)
    dmodel_dev = emb_all.shape[2]
    flat_emb = emb_all.reshape(requests * steps, dmodel_dev)
    xz_part = jnp.dot(
        flat_emb,
        w_xz.reshape(dmodel_dev, heads_dev * 2 * head_dim),
        preferred_element_type=jnp.float32,
    )
    xz_part = jnp.transpose(xz_part.reshape(requests, steps, heads_dev, 2 * head_dim), (0, 2, 1, 3))
    dt_part = jnp.dot(flat_emb, w_dt, preferred_element_type=jnp.float32)
    dt_part = jnp.transpose(dt_part.reshape(requests, steps, heads_dev), (0, 2, 1))
    bc_part = jnp.dot(flat_emb, w_bc, preferred_element_type=jnp.float32).reshape(
        requests, steps, w_bc.shape[1]
    )
    xz_heads, dt_heads, bc_heads = (
        lax.psum_scatter(xz_part, "dp", scatter_dimension=0, tiled=True),
        lax.psum_scatter(dt_part, "dp", scatter_dimension=0, tiled=True),
        lax.psum_scatter(bc_part, "dp", scatter_dimension=0, tiled=True),
    )
    bc_rows = lax.all_gather(bc_heads, "tensor", axis=2, tiled=True)
    state_quads = lax.all_to_all(
        arrange(state_heads, quads, RANKS), "tensor", split_axis=0, concat_axis=0, tiled=True
    )
    xz_quads, dt_quads = (
        lax.all_to_all(
            arrange(xz_heads, quads, RANKS), "tensor", split_axis=0, concat_axis=0, tiled=True
        ),
        lax.all_to_all(
            arrange(dt_heads, quads, RANKS), "tensor", split_axis=0, concat_axis=0, tiled=True
        ),
    )
    quad = tindex // RANKS
    rank = tindex % RANKS
    head_ids = (
        jnp.arange(ntensor)[:, None] * heads_dev
        + rank * rank_heads
        + jnp.arange(rank_heads)[None, :]
    )
    group_ids = head_ids // per_group
    all_bias, all_alog, all_skip, all_norm = (
        lax.all_gather(dt_bias, "tensor", axis=0, tiled=True),
        lax.all_gather(a_log, "tensor", axis=0, tiled=True),
        lax.all_gather(d_skip, "tensor", axis=0, tiled=True),
        lax.all_gather(norm_w, "tensor", axis=0, tiled=True),
    )

    def pick(values):
        shaped = values.reshape((ntensor, RANKS, rank_heads) + values.shape[1:])
        return lax.dynamic_index_in_dim(shaped, rank, 1, keepdims=False)

    bias_quad = pick(all_bias)[..., None]
    rate_quad = jnp.exp(pick(all_alog))[..., None]
    skip_quad = pick(all_skip)[..., None]
    norm_quad = pick(all_norm)
    my_rows = lax.dynamic_slice_in_dim(bc_rows, quad * group_req, group_req, 0).reshape(
        group_req, steps, GROUPS, 2 * state_dim
    )
    bc_quad = jnp.transpose(jnp.take(my_rows, group_ids, axis=2), (2, 3, 0, 1, 4))
    state_quads, gated = advance(
        state_quads, xz_quads, dt_quads, bc_quad, bias_quad, rate_quad, skip_quad
    )
    squares = jnp.sum(gated * gated, axis=-1)
    members = (group_ids[..., None] == jnp.arange(GROUPS)).astype(jnp.float32)
    grouped = jnp.einsum("tmjs,tmg->jsg", squares, members, precision=lax.Precision.HIGHEST)
    partial_value = lax.dynamic_update_slice_in_dim(
        jnp.zeros((req_dp, steps, GROUPS), jnp.float32), grouped, quad * group_req, 0
    )
    totals = group_totals(partial_value, RANKS.bit_length() - 1)
    mine_tot = lax.dynamic_slice_in_dim(totals, quad * group_req, group_req, 0)
    scale = lax.rsqrt(jnp.take(mine_tot, group_ids, axis=2) / (per_group * head_dim) + norm_eps)
    scale = jnp.transpose(scale, (2, 3, 0, 1))
    normed_quad = (gated * scale[..., None] * norm_quad[:, :, None, None, :]).astype(jnp.bfloat16)
    returned = lax.all_to_all(normed_quad, "tensor", split_axis=0, concat_axis=0, tiled=True)
    normed = restore(returned, quads, RANKS)
    decode_state = state_quads.reshape((1, 1, ntensor * rank_heads, group_req, head_dim, state_dim))
    mixed_in = jnp.transpose(normed, (0, 2, 1, 3)).reshape(req_dp, steps, heads_dev * head_dim)
    mix_all = jnp.einsum(
        "rsk,kd->rsd",
        lax.all_gather(mixed_in, "dp", axis=0, tiled=True),
        w_out,
        preferred_element_type=jnp.float32,
    )
    mix_mine = lax.psum_scatter(mix_all, "tensor", scatter_dimension=0, tiled=True)
    layer_out = (emb_mine + mix_mine).astype(jnp.bfloat16)
    return (layer_out, decode_state)


def solution(mesh):
    in_specs = (
        P("dp", "tensor", None, None),
        P(),
        P(),
        P("tensor", "dp"),
        P("dp", "tensor", None),
        P("dp", "tensor"),
        P("dp", "tensor"),
        P("tensor"),
        P("tensor"),
        P("tensor"),
        P("tensor", None),
        P("tensor", "dp"),
    )
    out_specs = (P("tensor", None, "dp"), P("dp", "tensor", None, None, None, None))
    return jax.shard_map(
        on_device, mesh=mesh, in_specs=in_specs, out_specs=out_specs, check_vma=False
    )
```

profile of v0, /device:TPU:0, one launch (start us, length us, event | category | flops | bytes accessed | tf_op | source)
XLA Modules:
  0.0 395.4 jit_solution(5296303745682983504)
XLA Ops:
  7.2 0.8 dynamic_slice.26
  8.0 0.7 sort.64
  8.8 5.0 %gather_fusion.4 = f32[4,32,64,128]{3,2,1,0:T(8,128)} fusion(f32[4,32,64,128]{3,2,1,0:T(8,128)} %param.14, s32[1024]{0:T(1024)S(1)} %pad_clamp_fusion.2), kind=kCustom, calls=%fused_computation.clone | custom fusion | bytes 8388624 | tf_op jit(solution)/shard_map/jit(_take)/gather | solution.py:72
  13.8 5.1 %select_bitcast_fusion = f32[4,1,32,64,128]{4,3,2,1,0:T(8,128)} fusion(f32[4,32,64,128]{3,2,1,0:T(8,128)} %gather_fusion.4, pred[4]{0:T(512)(128)(4,1)S(1)} %compare_and_fusion.2), kind=kLoop, calls=%fused_computation.9 | loop fusion | flops 1048576 | bytes 8388612 | tf_op jit(solution)/shard_map/reshape | solution.py:72
  18.9 5.3 %all-to-all-start = ((f32[4,1,32,64,128]{4,3,2,1,0:T(8,128)}), f32[4,1,32,64,128]{4,3,2,1,0:T(8,128)}, u32[]{:S(2)}, u32[]{:S(2)}) async-start(f32[4,1,32,64,128]{4,3,2,1,0:T(8,128)} %select_bitcast_fusion), calls=%async_computation | async-start | bytes 8388608 | tf_op jit(solution)/shard_map/all_to_all | solution.py:73
  24.2 1.2 sort.63
  25.6 0.6 gather_fusion
  26.6 2.4 gather_fusion.1
  29.2 0.3 select_convert_fusion
  29.5 0.7 copy.203
  30.4 17.4 %copy.289 = bf16[256,8,32,128]{3,1,2,0:T(8,128)(2,1)} copy(bf16[256,8,32,128]{3,2,1,0:T(8,128)(2,1)} %bitcast.127) | data formatting | bytes 33554432
  47.7 22.6 %copy.212 = bf16[4096,2048]{1,0:T(8,128)(2,1)} copy(bf16[4096,2048]{0,1:T(8,128)(2,1)} %bitcast.126) | data formatting | bytes 33554432 | tf_op jit(solution)/shard_map/dot_general | solution.py:119
  70.5 0.6 fusion.37
  71.7 0.6 sort.65
  72.3 0.7 sort.66
  73.1 14.4 %all-reduce.15.cloned.1.call-done = bf16[16,2,2048]{2,0,1:T(8,128)(2,1)} async-done(((bf16[16,2,2048]{2,0,1:T(8,128)(2,1)}), bf16[16,2,2048]{2,0,1:T(8,128)(2,1)}) %all-reduce.15.cloned.1.call-update) | async-done | bytes 131088
  87.5 0.9 constant_dynamic-slice_fusion.9
  88.4 14.0 %all_gather.21 = bf16[16,2,2048]{2,1,0:T(2,128)(2,1)S(1)} all-gather(bf16[2,2,2048]{2,1,0:T(2,128)(2,1)S(1)} %copy.206), channel_id=1, replica_groups=mesh['dp'=4,'tensor'=8] {'tensor'}, dimensions={0}, use_global_device_ids=true | all-gather | bytes 147456 | tf_op jit(solution)/shard_map/all_gather | solution.py:116
  102.4 8.6 %convolution_bitcast_fusion = f32[16,32,2,128]{3,0,1,2:T(8,128)S(1)} fusion(bf16[32,128,2048,1]{2,1,0,3:T(8,128)(2,1)} %bitcast.125, bf16[16,2,2048,1]{2,1,0,3:T(2,128)(2,1)S(1)} %bitcast.131), kind=kOutput, calls=%fused_computation.15 | convolution fusion | flops 536870912 | bytes 17432576 | tf_op jit(solution)/shard_map/dot_general | solution.py:119
  111.0 1.0 copy.214
  112.0 0.6 dynamic-slice.6
  113.4 0.3 fusion.2
  113.7 17.0 %all-reduce.11 = (f32[16,2,256]{2,0,1:T(8,128)S(1)}, f32[16,32,2]{1,0,2:T(8,128)S(1)}) all-reduce(f32[16,2,256]{2,0,1:T(8,128)S(1)} %fusion.2, f32[16,32,2]{1,0,2:T(8,128)S(1)} %convolution_bitcast_fusion.1), channel_id=5, replica_groups=mesh['dp'=4,'tensor'=8] {'dp'}, use_global_device_ids=true, to_apply=%region_7.9.clone | all-reduce | flops 9216 | bytes 73728
  130.8 0.6 copy.208
  131.4 3.3 all-to-all-start.2
  134.8 1.3 reduce-scatter.6.cloned.1.call-done
  136.1 0.9 copy.215
  137.0 0.7 copy.216
  137.7 5.0 %gather_fusion.5 = f32[4,32,64,128]{3,2,1,0:T(8,128)} fusion(f32[4,32,64,128]{3,2,1,0:T(8,128)} %bitcast.3, s32[1024]{0:T(1024)S(1)} %pad_clamp_fusion.1), kind=kCustom, calls=%fused_computation.1.clone | custom fusion | bytes 8388624 | tf_op jit(solution)/shard_map/jit(_take)/gather | solution.py:77
  142.7 4.6 %all-to-all-start.3 = ((f32[8,8,2,2,128]{4,2,1,3,0:T(2,128)}), f32[8,8,2,2,128]{4,2,1,3,0:T(2,128)S(1)}, u32[]{:S(2)}, u32[]{:S(2)}) async-start(f32[8,8,2,2,128]{4,2,1,3,0:T(2,128)} %copy.216), calls=%async_computation.4 | async-start | bytes 262144 | tf_op jit(solution)/shard_map/all_to_all | solution.py:140
  147.3 2.7 broadcast_select_fusion
  150.1 2.3 copy.205
  152.4 1.7 all-to-all-done.3
  154.1 4.7 %all-to-all-start.1 = ((f32[8,8,2,64,128]{4,3,2,1,0:T(8,128)}), f32[8,8,2,64,128]{4,3,2,1,0:T(8,128)}, u32[]{:S(2)}, u32[]{:S(2)}) async-start(f32[8,8,2,64,128]{4,3,2,1,0:T(8,128)} %bitcast.128), calls=%async_computation.1 | async-start | bytes 8388608 | tf_op jit(solution)/shard_map/all_to_all | solution.py:136
  160.7 107.2 %all-reduce.10 = (f32[8,4,8]{2,1,0:T(4,128)S(1)}, f32[8,4,8]{2,1,0:T(4,128)S(1)}, f32[8,4,8]{2,1,0:T(4,128)S(1)}) all-reduce(f32[8,4,8]{2,1,0:T(4,128)S(1)} %reshape.351, f32[8,4,8]{2,1,0:T(4,128)S(1)} %reshape.352, f32[8,4,8]{2,1,0:T(4,128)S(1)} %reshape.357), channel_id=1, replica_groups=mesh['dp'=4,'tensor'=8] {'tensor'}, use_global_device_ids=true, to_apply=%add | all-reduce | flops 768 | bytes 6144
  268.1 14.1 %all_gather.24 = f32[4,2,2048]{2,0,1:T(4,128)S(1)} all-gather(f32[4,2,256]{2,0,1:T(4,128)S(1)} %constant_dynamic-slice_fusion.7), channel_id=1, replica_groups=mesh['dp'=4,'tensor'=8] {'tensor'}, dimensions={2}, use_global_device_ids=true | all-gather | bytes 73728 | tf_op jit(solution)/shard_map/all_gather | solution.py:135
  282.3 0.9 gather_fusion.2
  284.4 8.5 %multiply_reduce_fusion = (f32[8,8,2,64]{3,2,1,0:T(2,128)S(1)}, f32[8,8,2,64,128]{4,3,2,1,0:T(8,128)}, f32[8,8,2,64]{3,2,1,0:T(2,128)S(1)}) fusion(f32[8,8,2,128]{3,2,1,0:T(2,128)S(1)} %copy.233, f32[8,8,2,128]{3,2,1,0:T(2,128)S(1)} %copy.232, f32[8,8,2,64]{3,2,1,0:T(2,128)S(1)} %copy.231, f32[8,8,2]{2,1,0:T(8,128)S(1)} %copy.228, ...), kind=kLoop, calls=%fused_computation.10 | loop fusion | flops 10469376 | bytes 8782848 | tf_op jit(solution)/shard_map/reduce_sum | solution.py:56
  293.4 0.3 collective-permute-start
  293.7 13.9 %all_gather.26 = f32[256,64]{1,0:T(8,128)S(1)} all-gather(f32[32,64]{1,0:T(8,128)S(1)} %copy-done.2), channel_id=1, replica_groups=mesh['dp'=4,'tensor'=8] {'tensor'}, dimensions={0}, use_global_device_ids=true | all-gather | bytes 73728 | tf_op jit(solution)/shard_map/all_gather | solution.py:159
  307.7 3.6 collective-permute-done.1
  311.4 0.7 gather_fusion.3
  312.5 8.1 %all_to_all.25 = bf16[8,2,1024]{2,1,0:T(2,128)(2,1)S(1)} all-to-all(bf16[8,2,1024]{2,1,0:T(2,128)(2,1)S(1)} %reshape.456), channel_id=1, replica_groups=mesh['dp'=4,'tensor'=8] {'tensor'}, dimensions={0} | all-to-all | bytes 65536 | tf_op jit(solution)/shard_map/all_to_all | solution.py:188
  320.9 8.4 %all_gather.27 = bf16[16,2,2048]{2,1,0:T(2,128)(2,1)S(1)} all-gather(bf16[4,2,2048]{2,1,0:T(2,128)(2,1)S(1)} %reshape.361), channel_id=1, replica_groups=mesh['dp'=4,'tensor'=8] {'dp'}, dimensions={0}, use_global_device_ids=true | all-gather | bytes 163840 | tf_op jit(solution)/shard_map/all_gather | solution.py:194
  329.3 5.6 %fusion = f32[16,2,2048]{2,0,1:T(8,128)} fusion(bf16[2048,2048]{1,0:T(8,128)(2,1)} %param.25, bf16[16,2,2048]{2,1,0:T(2,128)(2,1)S(1)} %all_gather.27), kind=kOutput, calls=%fused_computation.7 | convolution fusion | flops 268435456 | bytes 8781824 | tf_op jit(solution)/shard_map/rsk,kd->rsd/dot_general | solution.py:192
  334.9 52.4 %all-reduce.17.cloned.1.call-done = f32[16,2,2048]{2,0,1:T(8,128)} async-done(((f32[16,2,2048]{2,0,1:T(8,128)}), f32[16,2,2048]{2,0,1:T(8,128)}) %all-reduce.17.cloned.1.call-update) | async-done | bytes 262160
  387.4 0.9 fusion.11
  388.3 0.6 copy.243
  (118 shorter events, 5.1 us)
Async XLA Ops:
  7.2 106.3 %copy-start = (bf16[2048,256]{1,0:T(8,128)(2,1)S(1)}, bf16[2048,256]{1,0:T(8,128)(2,1)}, u32[]{:S(2)}) copy-start(bf16[2048,256]{1,0:T(8,128)(2,1)} %param.20) | copy-start | bytes 3145732
  18.9 5.3 %copy-start.5 = (s32[16]{0:T(128)S(1)}, s32[16]{0:T(128)}, u32[]{:S(2)}) copy-start(s32[16]{0:T(128)} %param.15) | copy-start | bytes 196
  18.9 6.6 %copy-start.4 = (s32[16,2]{0,1:T(2,128)S(1)}, s32[16,2]{0,1:T(2,128)}, u32[]{:S(2)}) copy-start(s32[16,2]{0,1:T(2,128)} %param.16) | copy-start | bytes 388
  18.9 112.5 %all-to-all-start = ((f32[4,1,32,64,128]{4,3,2,1,0:T(8,128)}), f32[4,1,32,64,128]{4,3,2,1,0:T(8,128)}, u32[]{:S(2)}, u32[]{:S(2)}) async-start(f32[4,1,32,64,128]{4,3,2,1,0:T(8,128)} %select_bitcast_fusion), calls=%async_computation | async-start | bytes 8388608 | tf_op jit(solution)/shard_map/all_to_all | solution.py:73
  24.2 63.3 %all-reduce.15.cloned.1.call-start = ((), (), s32[]{:S(2)}) async-start(), calls=%async_computation.7 | async-start | bytes 262144
  30.2 105.8 %reduce-scatter.6.cloned.1.call-start = ((), (), s32[]{:S(2)}) async-start(), calls=%async_computation.6 | async-start | bytes 655360 | tf_op jit(solution)/shard_map/reduce_scatter | solution.py:131
  47.7 22.7 %copy-start.3 = (u32[32]{0:T(128)S(1)}, u32[32]{0:T(128)}, u32[]{:S(2)}) copy-start(u32[32]{0:T(128)} %constant.153) | copy-start | bytes 388
  102.4 9.6 %copy-start.9 = (u32[32]{0:T(128)S(1)}, u32[32]{0:T(128)}, u32[]{:S(2)}) copy-start(u32[32]{0:T(128)} %constant.175) | copy-start | bytes 388
  102.4 10.9 %copy-start.1 = (bf16[2048,32]{0,1:T(8,128)(2,1)S(1)}, bf16[2048,32]{0,1:T(8,128)(2,1)}, u32[]{:S(2)}) copy-start(bf16[2048,32]{0,1:T(8,128)(2,1)} %param.19) | copy-start | bytes 393220
  131.4 11.3 %all-to-all-start.2 = ((f32[8,8,2,2]{1,3,2,0:T(2,128)}), f32[8,8,2,2]{1,3,2,0:T(2,128)S(1)}, u32[]{:S(2)}, u32[]{:S(2)}) async-start(f32[8,8,2,2]{1,3,2,0:T(2,128)} %bitcast.10), calls=%async_computation.2 | async-start | bytes 32768 | tf_op jit(solution)/shard_map/all_to_all | solution.py:143
  142.7 11.4 %all-to-all-start.3 = ((f32[8,8,2,2,128]{4,2,1,3,0:T(2,128)}), f32[8,8,2,2,128]{4,2,1,3,0:T(2,128)S(1)}, u32[]{:S(2)}, u32[]{:S(2)}) async-start(f32[8,8,2,2,128]{4,2,1,3,0:T(2,128)} %copy.216), calls=%async_computation.4 | async-start | bytes 262144 | tf_op jit(solution)/shard_map/all_to_all | solution.py:140
  154.1 5.3 %copy-start.6 = (f32[32]{0:T(128)S(1)}, f32[32]{0:T(128)}, u32[]{:S(2)}) copy-start(f32[32]{0:T(128)} %param.21) | copy-start | bytes 388
  154.1 5.7 %copy-start.7 = (f32[32]{0:T(128)S(1)}, f32[32]{0:T(128)}, u32[]{:S(2)}) copy-start(f32[32]{0:T(128)} %param.22) | copy-start | bytes 388
  154.1 6.1 %copy-start.8 = (f32[32]{0:T(128)S(1)}, f32[32]{0:T(128)}, u32[]{:S(2)}) copy-start(f32[32]{0:T(128)} %param.23) | copy-start | bytes 388
  154.1 130.2 %all-to-all-start.1 = ((f32[8,8,2,64,128]{4,3,2,1,0:T(8,128)}), f32[8,8,2,64,128]{4,3,2,1,0:T(8,128)}, u32[]{:S(2)}, u32[]{:S(2)}) async-start(f32[8,8,2,64,128]{4,3,2,1,0:T(8,128)} %bitcast.128), calls=%async_computation.1 | async-start | bytes 8388608 | tf_op jit(solution)/shard_map/all_to_all | solution.py:136
  158.8 228.6 %all-reduce.17.cloned.1.call-start = ((), (), s32[]{:S(2)}) async-start(), calls=%async_computation.8 | async-start | bytes 524288
  284.3 9.3 %copy-start.2 = (f32[32,64]{1,0:T(8,128)S(1)}, f32[32,64]{1,0:T(8,128)}, u32[]{:S(2)}) copy-start(f32[32,64]{1,0:T(8,128)} %param.24) | copy-start | bytes 24580
  293.4 14.3 %collective-permute-start = (f32[4,2,8]{2,1,0:T(2,128)S(1)}, f32[4,2,8]{2,1,0:T(2,128)S(1)}, u32[]{:S(2)}, u32[]{:S(2)}) collective-permute-start(f32[4,2,8]{2,1,0:T(2,128)S(1)} %get-tuple-element.54), channel_id=1, source_target_pairs={{0,1},{1,0},{2,3},{3,2},{4,5},{5,4},{6,7},{7,6},{8,9},{9,8},{10,11... | collective-permute-start | bytes 776 | tf_op jit(solution)/shard_map/ppermute | solution.py:17
  307.6 3.6 collective-permute-start.1
Sparse Core Ops, SparseCore 0:
  30.3 57.1 all-reduce.14
  112.1 23.9 reduce-scatter.5
  335.0 52.2 all-reduce.16
where the time goes:
time: 397 us; the launch traced here: 395 us
  blocking collectives  183 us (46%)
  waiting for transfers between devices  73.5 us (19%)
  local copies, waits for them, and re-layouts  67.9 us (17%)
  other arithmetic  21.9 us (6%)
  starting transfers between devices  18.3 us (5%)
  between operations  16.2 us (4%)
  matrix products  14.9 us (4%)
    unnamed x2, blocking collectives  124 us
    unnamed x5, waiting for transfers between devices  66.9 us
    dot_general x1, local copies, waits for them, and re-layouts, on_device(): jnp.dot(flat_emb, w_xz.reshape(dmodel_dev, heads_dev * 2 * head_dim), pre...  22.6 us
    unnamed x36, local copies, waits for them, and re-layouts  21.1 us
    all_gather x1, blocking collectives, on_device(): bc_rows = lax.all_gather(bc_heads, 'tensor', axis=2, tiled=True)  14.1 us
    all_gather x1, blocking collectives, on_device(): lax.all_gather(emb_mine.astype(jnp.bfloat16), 'tensor', axis=0, tiled=True)  14 us
    all_gather x1, blocking collectives, on_device(): lax.all_gather(norm_w, 'tensor', axis=0, tiled=True)  13.9 us
    dot_general x1, matrix products, on_device(): jnp.dot(flat_emb, w_xz.reshape(dmodel_dev, heads_dev * 2 * head_dim), pre...  8.59 us
  transfers between devices with their start and end apart: 9, of which 5 were waited for; matrix products, arithmetic and copies ran while one was open for 19% of the time, Pallas kernels for 0%

commit v1 on v0

--- a/solution.py
+++ b/solution.py
@@ -1,6 +1,8 @@
 import jax
 import jax.numpy as jnp
 from jax import lax
+from jax.experimental import pallas as pl
+from jax.experimental.pallas import tpu as pltpu
 from jax.sharding import PartitionSpec as P
 
 HEADS = 256
@@ -200,7 +202,413 @@
     return (layer_out, decode_state)
 
 
+def lookup_kernel(assign, tokens, table, emb, idx, inv, buf, rows32, sems):
+    d = lax.axis_index("dp")
+    t = lax.axis_index("tensor")
+    requests = assign.shape[0]
+    vocab_dev = table.shape[0]
+    req_dp = requests // lax.axis_size("dp")
+    nrows = buf.shape[0]
+    steps = tokens.shape[1]
+    for i in range(requests):
+        inv[assign[i]] = i
+    for i in range(req_dp):
+        idx[assign[d * req_dp + i] // req_dp] = i
+    for k in range(req_dp):
+        idx[req_dp + k] = inv[d * req_dp + k] // req_dp
+    local, copies = [], []
+    for row in range(nrows):
+        loc = tokens[inv[row // steps], row % steps] - t * vocab_dev
+        clipped = jnp.clip(loc, 0, vocab_dev - 1)
+        base = pl.multiple_of((clipped // 16) * 16, 16)
+        copy = pltpu.make_async_copy(table.at[pl.ds(base, 16), :], buf.at[row], sems.at[row])
+        copy.start()
+        copies.append(copy)
+        local.append(jnp.where(loc == clipped, clipped - base, -1))
+    sub = lax.broadcasted_iota(jnp.int32, (16, 1), 0)
+    for row in range(nrows):
+        copies[row].wait()
+        picked = jnp.where(sub == local[row], buf[row].astype(jnp.float32), 0.0)
+        rows32[row : row + 1, :] = jnp.sum(picked, axis=0, keepdims=True)
+    width = emb.shape[2]
+    for c in range(emb.shape[0]):
+        emb[c] = rows32[:, c * width : (c + 1) * width].astype(jnp.bfloat16)
+
+
+def split2(value):
+    high = value.astype(jnp.bfloat16).astype(jnp.float32)
+    return high, value - high
+
+
+def layer_kernel(
+    idx, embm, state, w_xz, w_bc, w_dt, bias, alog, skip, norm_w, w_out,
+    lo_out, ds_out,
+    state_v, wxz_v, wout_v, rsbuf, full, part, prx, snd1, arr0, arr1, arr2, arr3, stage, fin, sc, nall,
+    mix32, own32, mo, mrx, pk, pkrx, ost,
+    st_sem, w_sem, wo_sem, es_s, es_r, eg_s, eg_r, p1_s, p1_r, p2_s, p2_r,
+    x_s, x_r, n_s, n_r, k_s, k_r, m_s, m_r, o_sem,
+):
+    f32, bf16 = jnp.float32, jnp.bfloat16
+    d = lax.axis_index("dp")
+    t = lax.axis_index("tensor")
+    ND, NT = 4, 8
+    arr = (arr0, arr1, arr2, arr3)
+
+    def remote(src, dst, send, recv, axis, peer):
+        return pltpu.make_async_remote_copy(
+            src_ref=src, dst_ref=dst, send_sem=send, recv_sem=recv,
+            device_id={axis: peer}, device_id_type=pl.DeviceIdType.MESH,
+        )
+
+    st_copy = pltpu.make_async_copy(state, state_v, st_sem.at[0])
+    st_copy.start()
+
+    def w_copy(k):
+        rows = pl.ds(pl.multiple_of(k * 256, 256), 256)
+        return pltpu.make_async_copy(w_xz.at[rows], wxz_v.at[rows], w_sem.at[k])
+
+    for k in range(8):
+        w_copy(k).start()
+    wo_copy = pltpu.make_async_copy(w_out, wout_v, wo_sem.at[0])
+    wo_copy.start()
+
+    barrier = pltpu.get_barrier_semaphore()
+    for o in range(1, ND):
+        pl.semaphore_signal(barrier, inc=1, device_id={"dp": lax.rem(d + o, ND)},
+                            device_id_type=pl.DeviceIdType.MESH)
+    for o in range(1, NT):
+        pl.semaphore_signal(barrier, inc=1, device_id={"tensor": lax.rem(t + o, NT)},
+                            device_id_type=pl.DeviceIdType.MESH)
+    pl.semaphore_wait(barrier, ND + NT - 2)
+
+    sent = []
+    es = []
+    for o in range(1, NT):
+        peer = lax.rem(t + o, NT)
+        c = remote(embm.at[peer], rsbuf.at[o], es_s.at[o], es_r.at[o], "tensor", peer)
+        c.start()
+        es.append(c)
+    sent += es
+
+    st_copy.wait()
+    p1 = []
+
+    def send_chunk(m):
+        r = lax.rem(t + m, 4)
+        copies = []
+        for o in range(1, ND):
+            peer = lax.rem(d + o, ND)
+            snd1[peer, r] = state_v[idx[peer], r].astype(bf16)
+            c = remote(snd1.at[peer, r], arr[m].at[d], p1_s.at[m, o], p1_r.at[m, o], "dp", peer)
+            c.start()
+            copies.append(c)
+        arr[m][d] = state_v[idx[d], r].astype(bf16)
+        return copies
+
+    p1.append(send_chunk(0))
+    for c in es:
+        c.wait_recv()
+    total = embm[t].astype(f32)
+    for o in range(1, NT):
+        total = total + rsbuf[o].astype(f32)
+    full[t] = total.astype(bf16)
+    eg = []
+    for o in range(1, NT):
+        peer = lax.rem(t + o, NT)
+        c = remote(full.at[t], full.at[t], eg_s.at[o], eg_r.at[o], "tensor", peer)
+        c.start()
+        eg.append(c)
+    sent += eg
+    for m in range(1, 4):
+        p1.append(send_chunk(m))
+    for copies in p1:
+        sent += copies
+    for c in eg:
+        c.wait_recv()
+
+    def forward(m):
+        r = lax.rem(t + m, 4)
+        for c in p1[m]:
+            c.wait_recv()
+        for k in range(4):
+            stage[r, k] = arr[m][idx[4 + k]]
+        out = []
+        for o in (m, m + 4):
+            peer = lax.rem(t + o, NT)
+            first = pl.multiple_of((peer // 4) * 2, 2)
+            if o == 0:
+                for j in range(2):
+                    fin[0, j] = stage[r, first + j]
+                continue
+            c = remote(stage.at[r, pl.ds(first, 2)], fin.at[o], p2_s.at[o], p2_r.at[o], "tensor", peer)
+            c.start()
+            out.append((o, c))
+        return out
+
+    part[:, :, 4352:4480] = jnp.zeros((4, 8, 128), f32)
+    p2 = {}
+    for m in range(4):
+        for k in (2 * m, 2 * m + 1):
+            w_copy(k).wait()
+            e = full[k]
+            swapped = jnp.swapaxes(wxz_v[k * 256 : (k + 1) * 256], 0, 1)
+
+            def add(lo, width, value, first=(k == 0)):
+                value = value.reshape(4, 8, width)
+                if first and lo < 4352:
+                    part[:, :, lo : lo + width] = value
+                else:
+                    part[:, :, lo : lo + width] += value
+
+            for h in range(32):
+                add(h * 128, 128, jnp.dot(e, swapped[h], preferred_element_type=f32))
+            add(4096, 256, jnp.dot(e, w_bc[k * 256 : (k + 1) * 256, :], preferred_element_type=f32))
+            add(4352, 32, jnp.dot(e, w_dt[k * 256 : (k + 1) * 256, :], preferred_element_type=f32))
+        p2.update(dict(forward(m)))
+    sent += list(p2.values())
+
+    xs = []
+    for o in range(1, ND):
+        peer = lax.rem(d + o, ND)
+        c = remote(part.at[peer], prx.at[o], x_s.at[o], x_r.at[o], "dp", peer)
+        c.start()
+        xs.append(c)
+    sent += xs
+    for c in xs:
+        c.wait_recv()
+    proj = part[d] + prx[1] + prx[2] + prx[3]
+
+    low = lax.broadcasted_iota(jnp.int32, (8, 128), 1) < 64
+    xt, zt = [], []
+    for k in range(16):
+        a = proj[:, k * 256 : k * 256 + 128]
+        b = proj[:, k * 256 + 128 : k * 256 + 256]
+        xt.append(jnp.where(low, a, pltpu.roll(b, 64, 1)))
+        zt.append(jnp.where(low, pltpu.roll(a, 64, 1), b))
+    x = jnp.concatenate(xt, axis=1)
+    z = jnp.concatenate(zt, axis=1)
+    bc = proj[:, 4096:4352]
+    raw = proj[:, 4352:4384] + bias[...]
+    delta = jnp.maximum(raw, 0.0) + jnp.log1p(jnp.exp(-jnp.abs(raw)))
+    decay = jnp.exp(-delta * jnp.exp(alog[...]))
+    head_of = lax.broadcasted_iota(jnp.int32, (32, 2048), 1) // 64
+    spread = (head_of == lax.broadcasted_iota(jnp.int32, (32, 2048), 0)).astype(f32)
+    per_head = jnp.concatenate([delta, decay, jnp.broadcast_to(skip[...], (8, 32))], axis=0)
+    per_lane = jnp.dot(per_head, spread, precision=lax.Precision.HIGHEST, preferred_element_type=f32)
+
+    def step(value, s):
+        return jnp.concatenate([value[2 * k + s : 2 * k + s + 1] for k in range(4)], axis=0)
+
+    dx = per_lane[0:8] * x
+    x0, x1, z0, z1 = step(x, 0), step(x, 1), step(z, 0), step(z, 1)
+    u0, u1 = step(dx, 0), step(dx, 1)
+    a0, a1 = step(per_lane[8:16], 0), step(per_lane[8:16], 1)
+    sk = per_lane[16:20]
+    b0, b1 = step(bc[:, :128], 0), step(bc[:, :128], 1)
+    c0, c1 = step(bc[:, 128:], 0), step(bc[:, 128:], 1)
+    c0h, c0l = split2(c0)
+    c1h, c1l = split2(c1)
+    pad12 = jnp.zeros((12, 128), f32)
+    for k in range(4):
+        rows = [v[k : k + 1] for v in (c0h, c0l, c1h, c1l)]
+        cmat = jnp.concatenate(rows + [pad12], axis=0).astype(bf16)
+        for r in range(4):
+            prod = lax.dot_general(cmat, stage[r, k], (((1,), (1,)), ((), ())), preferred_element_type=f32)
+            sc[0, k : k + 1, r * 512 : (r + 1) * 512] = prod[0:1] + prod[1:2]
+            sc[1, k : k + 1, r * 512 : (r + 1) * 512] = prod[2:3] + prod[3:4]
+    b0c0 = jnp.sum(b0 * c0, axis=1, keepdims=True)
+    b0c1 = jnp.sum(b0 * c1, axis=1, keepdims=True)
+    b1c1 = jnp.sum(b1 * c1, axis=1, keepdims=True)
+    y0 = a0 * sc[0, 0:4, :] + u0 * b0c0 + sk * x0
+    y1 = a1 * (a0 * sc[1, 0:4, :] + u0 * b0c1) + u1 * b1c1 + sk * x1
+    g0 = y0 * (z0 * (1.0 / (1.0 + jnp.exp(-z0))))
+    g1 = y1 * (z1 * (1.0 / (1.0 + jnp.exp(-z1))))
+    width = g0.shape[1]
+
+    def norm(g):
+        ms = jnp.sum(g * g, axis=1, keepdims=True) / width
+        return g * lax.rsqrt(ms + norm_eps) * norm_w[...]
+
+    n0, n1 = norm(g0), norm(g1)
+    normed = jnp.concatenate([v[k : k + 1] for k in range(4) for v in (n0, n1)], axis=0)
+    nall[d] = jnp.concatenate([normed[:, :1024], normed[:, 1024:]], axis=0).astype(bf16)
+    ns = []
+    for o in range(1, ND):
+        peer = lax.rem(d + o, ND)
+        c = remote(nall.at[d], nall.at[d], n_s.at[o], n_r.at[o], "dp", peer)
+        c.start()
+        ns.append(c)
+    sent += ns
+
+    aa = a0 * a1
+    v0 = a1 * u0
+    pad256 = jnp.zeros((4, 256), f32)
+    bb = jnp.concatenate([b0, b1, pad256], axis=1)
+    for c in range(NT):
+        q, r = c // 4, c % 4
+        rows = []
+        for j in range(2):
+            k = 2 * q + j
+            for v in (v0, u1, aa):
+                rows.append(v[k : k + 1, r * 512 : (r + 1) * 512])
+            rows.append(bb[k : k + 1])
+        pk[c] = jnp.concatenate(rows, axis=0)
+    ks = {}
+    for o in range(1, NT):
+        peer = lax.rem(t + o, NT)
+        c = remote(pk.at[peer], pkrx.at[o], k_s.at[o], k_r.at[o], "tensor", peer)
+        c.start()
+        ks[o] = c
+    sent += list(ks.values())
+
+    for c in ns:
+        c.wait_recv()
+    blocks = []
+    for s in range(ND):
+        v = nall[s].astype(f32)
+        blocks.append(jnp.concatenate([v[0:8], v[8:16]], axis=1))
+    nmat = jnp.concatenate(blocks, axis=0).astype(bf16)
+    wo_copy.wait()
+    for q in range(4):
+        mix = jnp.dot(nmat, wout_v[:, q * 512 : (q + 1) * 512], preferred_element_type=f32)
+        emb = jnp.concatenate([full[2 * q], full[2 * q + 1]], axis=1).astype(f32)
+        mixed = mix + emb
+        for c in range(NT):
+            mix32[c, 4 * q : 4 * q + 4, :] = mix[4 * c : 4 * c + 4]
+            own32[c, 4 * q : 4 * q + 4, :] = mixed[4 * c : 4 * c + 4]
+    for c in range(NT):
+        mo[c] = mix32[c].astype(bf16)
+    ms = []
+    for o in range(1, NT):
+        peer = lax.rem(t + o, NT)
+        c = remote(mo.at[peer], mrx.at[o], m_s.at[o], m_r.at[o], "tensor", peer)
+        c.start()
+        ms.append(c)
+    sent += ms
+
+    def finish(o):
+        source = lax.rem(t + NT - o, NT)
+        if o == 0:
+            pack = pk[t]
+        else:
+            p2[o].wait_recv()
+            ks[o].wait_recv()
+            pack = pkrx[o]
+        for j in range(2):
+            uh, ul = split2(pack[4 * j : 4 * j + 1])
+            wh, wl = split2(pack[4 * j + 1 : 4 * j + 2])
+            ah, al = split2(pack[4 * j + 2 : 4 * j + 3])
+            bh, bl = split2(pack[4 * j + 3 : 4 * j + 4])
+            left = jnp.concatenate(
+                [uh, uh, ul, wh, wh, wl, ah, al, jnp.zeros((8, 512), f32)], axis=0
+            ).astype(bf16)
+            b0h, b0l, b1h, b1l = bh[:, :128], bl[:, :128], bh[:, 128:256], bl[:, 128:256]
+            outer = jnp.concatenate(
+                [b0h, b0l, b0h, b1h, b1l, b1h, jnp.zeros((10, 128), f32)], axis=0
+            ).astype(bf16)
+            row = lax.broadcasted_iota(jnp.int32, (16, 128), 0)
+            ones = jnp.where((row == 6) | (row == 7), 1.0, 0.0).astype(bf16)
+            right = jnp.concatenate([ones, outer], axis=1)
+            g = lax.dot_general(left, right, (((0,), (0,)), ((), ())), preferred_element_type=f32)
+            new = fin[o, j].astype(f32) * g[:, :128] + g[:, 128:]
+            ost[o, :, j] = new.reshape(8, 64, 128)
+        c = pltpu.make_async_copy(ost.at[o], ds_out.at[source], o_sem.at[o])
+        c.start()
+        return c
+
+    outs = [finish(0)]
+    for c in ms:
+        c.wait_recv()
+    own = own32[t]
+    for o in range(1, NT):
+        own = own + mrx[o].astype(f32)
+    lo_out[...] = jnp.concatenate([own[4 * q : 4 * q + 4] for q in range(4)], axis=1).astype(bf16)
+    for o in (4, 1, 5, 2, 6, 3, 7):
+        outs.append(finish(o))
+    for c in sent:
+        c.wait_send()
+    for c in outs:
+        c.wait()
+
+
+def fused(
+    prefill_state, assign, tokens, embed_table, w_xz, w_dt, w_bc, dt_bias, a_log, d_skip, norm_w, w_out
+):
+    f32, bf16 = jnp.float32, jnp.bfloat16
+    vmem = pl.BlockSpec(memory_space=pltpu.VMEM)
+    smem = pl.BlockSpec(memory_space=pltpu.SMEM)
+    hbm = pl.BlockSpec(memory_space=pl.ANY)
+    embm, idx = pl.pallas_call(
+        lookup_kernel,
+        out_shape=(
+            jax.ShapeDtypeStruct((8, 32, 256), bf16),
+            jax.ShapeDtypeStruct((8,), jnp.int32),
+        ),
+        in_specs=[smem, smem, hbm],
+        out_specs=(vmem, smem),
+        scratch_shapes=[
+            pltpu.SMEM((16,), jnp.int32),
+            pltpu.VMEM((32, 16, 2048), bf16),
+            pltpu.VMEM((32, 2048), f32),
+            pltpu.SemaphoreType.DMA((32,)),
+        ],
+        compiler_params=pltpu.CompilerParams(vmem_limit_bytes=8 << 20),
+    )(assign, tokens, embed_table)
+    dma = pltpu.SemaphoreType.DMA
+    layer_out, decode_state = pl.pallas_call(
+        layer_kernel,
+        out_shape=(
+            jax.ShapeDtypeStruct((4, 2048), bf16),
+            jax.ShapeDtypeStruct((8, 8, 2, 64, 128), f32),
+        ),
+        in_specs=[smem, vmem, hbm, hbm, vmem, vmem, vmem, vmem, vmem, vmem, hbm],
+        out_specs=(vmem, hbm),
+        scratch_shapes=[
+            pltpu.VMEM((4, 4, 512, 128), f32),
+            pltpu.VMEM((2048, 32, 128), bf16),
+            pltpu.VMEM((2048, 2048), bf16),
+            pltpu.VMEM((8, 32, 256), bf16),
+            pltpu.VMEM((8, 32, 256), bf16),
+            pltpu.VMEM((4, 8, 4480), f32),
+            pltpu.VMEM((4, 8, 4480), f32),
+            pltpu.VMEM((4, 4, 512, 128), bf16),
+            pltpu.VMEM((4, 512, 128), bf16),
+            pltpu.VMEM((4, 512, 128), bf16),
+            pltpu.VMEM((4, 512, 128), bf16),
+            pltpu.VMEM((4, 512, 128), bf16),
+            pltpu.VMEM((4, 4, 512, 128), bf16),
+            pltpu.VMEM((8, 2, 512, 128), bf16),
+            pltpu.VMEM((2, 8, 2048), f32),
+            pltpu.VMEM((4, 16, 1024), bf16),
+            pltpu.VMEM((8, 16, 512), f32),
+            pltpu.VMEM((8, 16, 512), f32),
+            pltpu.VMEM((8, 16, 512), bf16),
+            pltpu.VMEM((8, 16, 512), bf16),
+            pltpu.VMEM((8, 8, 512), f32),
+            pltpu.VMEM((8, 8, 512), f32),
+            pltpu.VMEM((8, 8, 2, 64, 128), f32),
+            dma((1,)), dma((8,)), dma((1,)),
+            dma((8,)), dma((8,)), dma((8,)), dma((8,)),
+            dma((4, 4)), dma((4, 4)), dma((8,)), dma((8,)),
+            dma((4,)), dma((4,)), dma((4,)), dma((4,)),
+            dma((8,)), dma((8,)), dma((8,)), dma((8,)), dma((8,)),
+        ],
+        compiler_params=pltpu.CompilerParams(
+            collective_id=0, has_side_effects=True, vmem_limit_bytes=60 << 20
+        ),
+        cost_estimate=pl.CostEstimate(
+            flops=900_000_000, bytes_accessed=40_000_000, transcendentals=100_000
+        ),
+    )(
+        idx, embm, prefill_state.reshape(4, 4, 512, 128), w_xz, w_bc, w_dt,
+        dt_bias.reshape(1, 32), a_log.reshape(1, 32), d_skip.reshape(1, 32),
+        norm_w.reshape(1, 2048), w_out,
+    )
+    return layer_out.reshape(2, 2, 2048), decode_state.reshape(1, 1, 64, 2, 64, 128)
+
+
 def solution(mesh):
+    sizes = (mesh.shape["dp"], mesh.shape["tensor"])
     in_specs = (
         P("dp", "tensor", None, None),
         P(),
@@ -217,5 +625,5 @@
     )
     out_specs = (P("tensor", None, "dp"), P("dp", "tensor", None, None, None, None))
     return jax.shard_map(
-        on_device, mesh=mesh, in_specs=in_specs, out_specs=out_specs, check_vma=False
-    )
+        fused if sizes == (4, 8) else on_device, mesh=mesh, in_specs=in_specs, out_specs=out_specs, check_vma=False
+    )

time: 397 us -> 104 us (0.26)
  blocking collectives: 183 us -> 0 us
  Pallas kernels: 0 us -> 81.1 us
  waiting for transfers between devices: 73.5 us -> 0 us
  local copies, waits for them, and re-layouts: 67.9 us -> 21.6 us
  other arithmetic: 21.9 us -> 0 us
  starting transfers between devices: 18.3 us -> 0 us
  between operations: 16.2 us -> 0.66 us
  matrix products: 14.9 us -> 0 us
    unnamed x2 -> x0, blocking collectives: 124 us -> none
    pallas_call x0 -> x2, Pallas kernels: none -> 81.1 us  [the longest x1 75.3 us: fused(): pl.pallas_call(layer_kernel, out_shape=(jax.ShapeDtypeStruct((4, 2048), b...]
    unnamed x5 -> x0, waiting for transfers between devices: 66.9 us -> none
    all_gather x4 -> x0, blocking collectives: 50.4 us -> none  [the longest x1 14.1 us: on_device(): bc_rows = lax.all_gather(bc_heads, 'tensor', axis=2, tiled=True)]
    dot_general x1 -> x0, local copies, waits for them, and re-layouts: 22.6 us -> none  [on_device(): jnp.dot(flat_emb, w_xz.reshape(dmodel_dev, heads_dev * 2 * head_dim), pre...]
    all_to_all x4 -> x0, starting transfers between devices: 17.9 us -> none  [the longest x1 5.29 us: to_groups(): lax.all_to_all(outgoing, 'dp', split_axis=0, concat_axis=0, tiled=True)]
    dot_general x5 -> x0, matrix products: 14.9 us -> none  [the longest x1 8.59 us: on_device(): jnp.dot(flat_emb, w_xz.reshape(dmodel_dev, heads_dev * 2 * head_dim), pre...]
    gather x9 -> x0, local copies, waits for them, and re-layouts: 14.9 us -> none  [the longest x1 5.02 us: to_groups(): jnp.take(state, send_order, axis=0).reshape((ndp, pair) + state.shape[1:])]
  transfers between devices with their start and end apart: 9 -> 0, of which waited for: 5 -> 0; matrix products, arithmetic and copies ran while one was open for 19% -> 0% of each run, Pallas kernels for 0% -> 0%
where the time goes in v1:
time: 104 us; the launch traced here: 103 us
  Pallas kernels  81.1 us (78%)
  local copies, waits for them, and re-layouts  21.6 us (21%)
    pallas_call x1, Pallas kernels, fused(): pl.pallas_call(layer_kernel, out_shape=(jax.ShapeDtypeStruct((4, 2048), b...  75.3 us
    unnamed x13, local copies, waits for them, and re-layouts  18.9 us
    pallas_call x1, Pallas kernels, fused(): pl.pallas_call(lookup_kernel, out_shape=(jax.ShapeDtypeStruct((8, 32, 256...  5.87 us

profile of v1, /device:TPU:0, one launch (start us, length us, event | category | flops | bytes accessed | tf_op | source)
XLA Modules:
  0.0 103.4 jit_solution(9082833962646701959)
XLA Ops:
  0.6 0.8 copy.14.tokens
  1.4 1.4 %reshape.29.norm_w = f32[1,2048]{1,0:T(1,128)} reshape(f32[32,64]{1,0:T(8,128)} %param.22) | data formatting | bytes 16384 | tf_op jit(solution)/shard_map/reshape | solution.py:605
  2.8 0.0 copy-start
  2.8 10.5 %copy-done = bf16[8192,2048]{1,0:T(8,128)(2,1)S(1)} copy-done((bf16[8192,2048]{1,0:T(8,128)(2,1)S(1)}, bf16[8192,2048]{1,0:T(8,128)(2,1)}, u32[]{:S(2)}) %copy-start) | copy-done | bytes 33554456
  13.3 0.0 copy-start.2
  13.3 0.7 copy-done.2
  14.0 0.0 copy-start.4
  14.0 5.9 %shard_map.131 = (bf16[8,32,256]{2,1,0:T(8,128)(2,1)S(1)}, s32[8]{0:T(128)S(1)}) custom-call(s32[16]{0:T(128)S(1)} %copy-done.2, s32[16,2]{1,0:T(8,128)S(1)} %copy.14.tokens, bf16[8192,2048]{1,0:T(8,128)(2,1)S(1)} %copy-done), custom_call_target="tpu_custom_call" | custom-call | tf_op jit(solution)/shard_map/pallas_call | solution.py:541
  19.9 0.0 copy-start.1
  19.9 0.6 copy-done.1
  20.5 0.0 copy-start.3
  20.5 0.5 copy-done.3
  21.0 0.0 copy-done.4
  21.0 1.0 copy.15.w_dt
  22.0 75.3 %shard_map.132 = (bf16[4,2048]{1,0:T(4,128)(2,1)}, f32[8,8,2,64,128]{4,3,2,1,0:T(8,128)}) custom-call(s32[8]{0:T(128)} %copy-done.3, bf16[8,32,256]{2,1,0:T(8,128)(2,1)} %copy-done.1, f32[4,4,512,128]{3,2,1,0:T(8,128)} %bitcast.5, bf16[2048,32,128]{2,1,0:T(8,128)(2,1)} %w_xz.1, bf16[2048,256]{1,0:T(8,128)(2,1)} %w_bc.1, bf16[2048,32]{1,0:T(8,128)(2,1)} %copy.15.w_dt, ...), custom_call_target="tpu_custom_call" | custom-call | flops 900000000 | bytes 40000000 | tf_op jit(solution)/shard_map/pallas_call | solution.py:558
  97.3 1.3 %reshape.30 = bf16[2,2,2048]{2,1,0:T(2,128)(2,1)} reshape(bf16[4,2048]{1,0:T(4,128)(2,1)} %get-tuple-element.8) | data formatting | bytes 32768 | tf_op jit(solution)/shard_map/reshape | solution.py:607
  98.6 4.8 %copy.17 = f32[1,1,64,2,64,128]{5,4,3,2,1,0:T(8,128)} copy(f32[1,1,64,2,64,128]{5,4,3,2,1,0:T(8,128)} %bitcast.6) | data formatting | bytes 8388608
Async XLA Ops:
  2.8 10.5 %copy-start = (bf16[8192,2048]{1,0:T(8,128)(2,1)S(1)}, bf16[8192,2048]{1,0:T(8,128)(2,1)}, u32[]{:S(2)}) copy-start(bf16[8192,2048]{1,0:T(8,128)(2,1)} %table.1) | copy-start | bytes 100663296
  13.3 0.7 copy-start.2
  14.0 7.0 %copy-start.4 = (bf16[2048,32]{0,1:T(8,128)(2,1)S(1)}, bf16[2048,32]{0,1:T(8,128)(2,1)}, u32[]{:S(2)}) copy-start(bf16[2048,32]{0,1:T(8,128)(2,1)} %param.17) | copy-start | bytes 393220
  19.9 0.6 copy-start.1
  20.5 0.5 copy-start.3

commit v2 on v1

--- a/solution.py
+++ b/solution.py
@@ -516,14 +516,14 @@
         c.start()
         return c
 
-    outs = [finish(0)]
+    outs = [finish(o) for o in (0, 4, 1, 5)]
     for c in ms:
         c.wait_recv()
     own = own32[t]
     for o in range(1, NT):
         own = own + mrx[o].astype(f32)
     lo_out[...] = jnp.concatenate([own[4 * q : 4 * q + 4] for q in range(4)], axis=1).astype(bf16)
-    for o in (4, 1, 5, 2, 6, 3, 7):
+    for o in (2, 6, 3, 7):
         outs.append(finish(o))
     for c in sent:
         c.wait_send()
@@ -552,7 +552,7 @@
             pltpu.VMEM((32, 2048), f32),
             pltpu.SemaphoreType.DMA((32,)),
         ],
-        compiler_params=pltpu.CompilerParams(vmem_limit_bytes=8 << 20),
+        compiler_params=pltpu.CompilerParams(vmem_limit_bytes=60 << 20),
     )(assign, tokens, embed_table)
     dma = pltpu.SemaphoreType.DMA
     layer_out, decode_state = pl.pallas_call(

time: 104 us -> 90 us (0.87)
  local copies, waits for them, and re-layouts: 21.6 us -> 9.87 us
  Pallas kernels: 81.1 us -> 78.8 us
    unnamed x13 -> x5, local copies, waits for them, and re-layouts: 18.9 us -> 7.15 us
    pallas_call x1, Pallas kernels: 75.3 us -> 74 us  [fused(): pl.pallas_call(layer_kernel, out_shape=(jax.ShapeDtypeStruct((4, 2048), b...]
    pallas_call x1, Pallas kernels: 5.87 us -> 4.73 us  [fused(): pl.pallas_call(lookup_kernel, out_shape=(jax.ShapeDtypeStruct((8, 32, 256...]
where the time goes in v2:
time: 90 us; the launch traced here: 89.3 us
  Pallas kernels  78.8 us (88%)
  local copies, waits for them, and re-layouts  9.87 us (11%)
    pallas_call x1, Pallas kernels, fused(): pl.pallas_call(layer_kernel, out_shape=(jax.ShapeDtypeStruct((4, 2048), b...  74 us
    unnamed x5, local copies, waits for them, and re-layouts  7.15 us
    pallas_call x1, Pallas kernels, fused(): pl.pallas_call(lookup_kernel, out_shape=(jax.ShapeDtypeStruct((8, 32, 256...  4.73 us

profile of v2, /device:TPU:0, one launch (start us, length us, event | category | flops | bytes accessed | tf_op | source)
XLA Modules:
  0.0 89.3 jit_solution(891542094811074007)
XLA Ops:
  0.6 1.4 %copy.14.tokens = s32[16,2]{1,0:T(8,128)} copy(s32[16,2]{0,1:T(2,128)} %param.14) | data formatting | bytes 256 | tf_op args[2]
  2.0 1.4 %reshape.29.norm_w = f32[1,2048]{1,0:T(1,128)} reshape(f32[32,64]{1,0:T(8,128)} %param.22) | data formatting | bytes 16384 | tf_op jit(solution)/shard_map/reshape | solution.py:605
  3.4 0.0 copy-start
  3.4 4.7 %shard_map.131 = (bf16[8,32,256]{2,1,0:T(8,128)(2,1)}, s32[8]{0:T(128)}) custom-call(s32[16]{0:T(128)} %assign.1, s32[16,2]{1,0:T(8,128)} %copy.14.tokens, bf16[8192,2048]{1,0:T(8,128)(2,1)} %table.1), custom_call_target="tpu_custom_call" | custom-call | tf_op jit(solution)/shard_map/pallas_call | solution.py:541
  8.1 0.0 copy-done
  8.1 1.0 %copy.15.w_dt = bf16[2048,32]{1,0:T(8,128)(2,1)} copy(bf16[2048,32]{0,1:T(8,128)(2,1)S(1)} %copy-done) | data formatting | bytes 262144 | tf_op args[5]
  9.1 74.0 %shard_map.132 = (bf16[4,2048]{1,0:T(4,128)(2,1)}, f32[8,8,2,64,128]{4,3,2,1,0:T(8,128)}) custom-call(s32[8]{0:T(128)} %get-tuple-element.6.idx, bf16[8,32,256]{2,1,0:T(8,128)(2,1)} %get-tuple-element.7.embm, f32[4,4,512,128]{3,2,1,0:T(8,128)} %bitcast.5, bf16[2048,32,128]{2,1,0:T(8,128)(2,1)} %w_xz.1, bf16[2048,256]{1,0:T(8,128)(2,1)} %w_bc.1, ...), custom_call_target="tpu_custom_call" | custom-call | flops 900000000 | bytes 40000000 | tf_op jit(solution)/shard_map/pallas_call | solution.py:558
  83.2 1.3 %reshape.30 = bf16[2,2,2048]{2,1,0:T(2,128)(2,1)} reshape(bf16[4,2048]{1,0:T(4,128)(2,1)} %get-tuple-element.8) | data formatting | bytes 32768 | tf_op jit(solution)/shard_map/reshape | solution.py:607
  84.5 4.8 %copy.17 = f32[1,1,64,2,64,128]{5,4,3,2,1,0:T(8,128)} copy(f32[1,1,64,2,64,128]{5,4,3,2,1,0:T(8,128)} %bitcast.6) | data formatting | bytes 8388608
Async XLA Ops:
  3.4 4.7 %copy-start = (bf16[2048,32]{0,1:T(8,128)(2,1)S(1)}, bf16[2048,32]{0,1:T(8,128)(2,1)}, u32[]{:S(2)}) copy-start(bf16[2048,32]{0,1:T(8,128)(2,1)} %param.17) | copy-start | bytes 393220
